TPU v7x, 32 devices: a whole 2x2x4 slice. The times are simulated.
32 devices in a mesh: dp: 8 (over z, core), tensor: 4 (over y, x).
Axes of the slice: x: 2, y: 2, z: 4, core: 2. Of those that a mesh axis runs over, the one named last changes fastest.
Arguments:
- hidden_in: bfloat16 [8192, 2048], P(('dp', 'tensor')), may hold values from -6 to 6
- doc_lengths: int32 [8, 8], P('dp'), may hold values from 1 to 512, 1024 in all within a row
- gain_attn: bfloat16 [2048], P('dp'), may hold values from 0.099609375 to 1.8984375
- w_query: bfloat16 [2048, 2048], P('dp', 'tensor'), may hold values from -0.125 to 0.125
- w_key: bfloat16 [2048, 2048], P('dp', 'tensor'), may hold values from -0.125 to 0.125
- w_value: bfloat16 [2048, 2048], P('dp', 'tensor'), may hold values from -0.125 to 0.125
- w_out: bfloat16 [2048, 2048], P('tensor', 'dp'), may hold values from -1 to 1
- gain_mlp: bfloat16 [2048], P('dp'), may hold values from 0.099609375 to 1.8984375
- w_gate: bfloat16 [2048, 8192], P('dp', 'tensor'), may hold values from -0.125 to 0.125
- w_up: bfloat16 [2048, 8192], P('dp', 'tensor'), may hold values from -0.125 to 0.125
- w_down: bfloat16 [8192, 2048], P('tensor', 'dp'), may hold values from -0.125 to 0.125
- cotangent: bfloat16 [8192, 2048], P(('dp', 'tensor')), may hold values from -16 to 16
Outputs:
- output: bfloat16 [8192, 2048], P(('dp', 'tensor'))
- input_grad: float32 [8192, 2048], P(('dp', 'tensor'))
- grad_gain_attn: float32 [2048], P(('dp', 'tensor'))
- grad_query: float32 [2048, 2048], P('dp', 'tensor')
- grad_key: float32 [2048, 2048], P('dp', 'tensor')
- grad_value: float32 [2048, 2048], P('dp', 'tensor')
- grad_out: float32 [2048, 2048], P('tensor', 'dp')
- grad_gain_mlp: float32 [2048], P(('dp', 'tensor'))
- grad_gate: float32 [2048, 8192], P('dp', 'tensor')
- grad_up: float32 [2048, 8192], P('dp', 'tensor')
- grad_down: float32 [8192, 2048], P('tensor', 'dp')
Inputs may be any that keep to these rules, and one draw needn't show every extreme that they name: `doc_lengths`: each row holds the lengths of the 8 documents of one packed sequence in order; a row sums to 1024 and its largest length is exactly 512.
All inputs are finite; a program needn't handle non-finite values.
Results may differ from a plain program's by a relative error of at most 0.02.
Values may be sent and summed in bfloat16 or wider, within the bound.
A program may use at most 256 MiB of HBM per device.

v0:
```python
import functools
import math

import jax
import jax.numpy as jnp
from jax import lax
from jax.experimental import pallas as pl
from jax.experimental.pallas import tpu as pltpu
from jax.sharding import PartitionSpec as P

HEAD_DIM = 64
LEN = 1024
MOST = 512
EPSILON = 1e-05
ROPE_BASE = 130000.0
NEG = -1e30
GROUP = 256
FF_BLOCKS = 8
F32 = jnp.float32
BF16 = jnp.bfloat16
VMEM_BYTES = 63 * 1024 * 1024


def dot_nn(a, b):
    return jnp.dot(a, b, preferred_element_type=F32)


def dot_tn(a, b):
    return lax.dot_general(a, b, (((0,), (0,)), ((), ())), preferred_element_type=F32)


def dot_nt(a, b):
    return lax.dot_general(a, b, (((1,), (1,)), ((), ())), preferred_element_type=F32)


def norm_factor(values):
    return lax.rsqrt(jnp.mean(values * values, axis=-1, keepdims=True) + EPSILON)


def norm_back(values, factor, gain, grads):
    scaled = grads * gain
    grad_in = factor * scaled - values * factor * factor * factor * jnp.mean(
        scaled * values, axis=-1, keepdims=True
    )
    return grad_in, jnp.sum(grads * values * factor, axis=0)


def doc_tables(doc_lengths, tokens):
    ends = jnp.cumsum(doc_lengths, axis=1)[0]
    passed = tokens[:, None] >= ends[None, :]
    segment = jnp.sum(passed.astype(jnp.int32), axis=1)
    start = jnp.sum(jnp.where(passed, doc_lengths, 0), axis=1)
    return segment, tokens - start


def rotary_tables(position):
    half = HEAD_DIM // 2
    inverse = jnp.power(ROPE_BASE, -jnp.arange(half, dtype=F32) * 2.0 / HEAD_DIM)
    angles = position.astype(F32)[:, None] * inverse
    cosine, sine = jnp.cos(angles), jnp.sin(angles)
    heads = 128 // HEAD_DIM
    return (
        jnp.tile(jnp.concatenate([cosine, cosine], axis=1), (1, heads)),
        jnp.tile(jnp.concatenate([-sine, sine], axis=1), (1, heads)),
    )


def swap_halves(v):
    half, width = HEAD_DIM // 2, v.shape[1]
    lane = lax.broadcasted_iota(jnp.int32, v.shape, 1)
    ahead = pltpu.roll(v, width - half, 1)
    behind = pltpu.roll(v, half, 1)
    return jnp.where(lane % HEAD_DIM < half, ahead, behind)


def key_blocks(i, rows):
    reach = -(-(MOST - 1) // rows)
    return list(range(max(0, i - reach), i + 1))


def fill_bias(bias_ref, seg_col, seg_ref, i, places):
    rows = seg_col.shape[0]
    for n, (j, place) in enumerate(places):
        same = seg_col == seg_ref[place][0:1, :]
        if j == i:
            row = lax.broadcasted_iota(jnp.int32, (rows, rows), 0)
            col = lax.broadcasted_iota(jnp.int32, (rows, rows), 1)
            same = same & (col <= row)
        bias_ref[n] = jnp.where(same, 0.0, NEG)


def attn_forward_kernel(
    blocks, key_ref, x_ref, qo, qs, ko, ks, vo, vs, cos_ref, sin_ref, segc_ref, segr_ref,
    q_ref, k_ref, v_ref, mixed_ref, lse_ref, bias_ref,
):
    rows = LEN // blocks
    half = x_ref.shape[1] // 2
    key = key_ref[0]

    @pl.loop(0, blocks)
    def _(b):
        at = pl.ds(pl.multiple_of(b * rows, rows), rows)
        left, right = x_ref[at, :half], x_ref[at, half:]
        cosine, sine = cos_ref[at, :], sin_ref[at, :]
        query = dot_nn(left, qo[...]) + dot_nn(right, qs[...])
        q_ref[at, :] = (query * cosine + swap_halves(query) * sine).astype(BF16)
        keys = dot_nn(left, ko[...]) + dot_nn(right, ks[...])
        k_ref[at, :] = (keys * cosine + swap_halves(keys) * sine).astype(BF16)
        v_ref[at, :] = (dot_nn(left, vo[...]) + dot_nn(right, vs[...])).astype(BF16)

    head_lane = lax.broadcasted_iota(jnp.int32, (rows, 128), 1)
    for i in range(blocks):
        places = [(j, j ^ key) for j in key_blocks(i, rows)]
        at = pl.ds(pl.multiple_of((i ^ key) * rows, rows), rows)
        fill_bias(bias_ref, segc_ref[at, 0:1], segr_ref, i, places)
        spots = [pl.ds(pl.multiple_of(p * rows, rows), rows) for _, p in places]

        @pl.loop(0, GROUP // 128)
        def _(pair, at=at, spots=spots):
            first = pl.program_id(0) * (GROUP // HEAD_DIM)
            attend(pair, first, at, spots, head_lane, q_ref, k_ref, v_ref, mixed_ref, lse_ref, bias_ref)


def attn_forward(blocks, key, x, own, sib, cosine, sine, segc, segr):
    d = x.shape[1]
    cols = own.shape[1] // 3
    steps = cols // GROUP
    rows = LEN // blocks

    def weight(part):
        return pl.BlockSpec((d // 2, GROUP), lambda i, part=part: (0, part * steps + i))

    def whole(shape):
        return pl.BlockSpec(shape, lambda i: (0,) * len(shape))

    col_block = pl.BlockSpec((LEN, GROUP), lambda i: (0, i))
    slab = jax.ShapeDtypeStruct((LEN, cols), BF16)
    return pl.pallas_call(
        functools.partial(attn_forward_kernel, blocks),
        grid=(steps,),
        in_specs=[pl.BlockSpec(memory_space=pltpu.SMEM), whole((LEN, d))]
        + [weight(p) for p in (0, 0, 1, 1, 2, 2)]
        + [whole((LEN, GROUP))] * 2
        + [whole((LEN, 128)), whole(segr.shape)],
        out_specs=[col_block] * 4 + [whole((LEN, 128))],
        out_shape=[slab] * 4 + [jax.ShapeDtypeStruct((LEN, 128), F32)],
        scratch_shapes=[pltpu.VMEM((blocks, rows, rows), F32)],
        compiler_params=pltpu.CompilerParams(vmem_limit_bytes=VMEM_BYTES),
        name="attn_forward",
    )(key, x, own, sib, own, sib, own, sib, cosine, sine, segc, segr)


def attn_backward_kernel(
    blocks, key_ref, g_ref, wo, ws, q_ref, k_ref, v_ref, lse_ref, cos_ref, sin_ref, segc_ref,
    segr_ref, dq_ref, dk_ref, dv_ref, dm_ref, dqa_ref, dka_ref, dva_ref, bias_ref,
):
    rows = LEN // blocks
    half = g_ref.shape[1] // 2
    key = key_ref[0]

    @pl.loop(0, blocks)
    def _(b):
        at = pl.ds(pl.multiple_of(b * rows, rows), rows)
        dm_ref[at, :] = (dot_nn(g_ref[at, :half], wo[...]) + dot_nn(g_ref[at, half:], ws[...])).astype(BF16)
        dka_ref[at, :] = jnp.zeros((rows, GROUP), F32)
        dva_ref[at, :] = jnp.zeros((rows, GROUP), F32)

    head_lane = lax.broadcasted_iota(jnp.int32, (rows, 128), 1)
    scale = HEAD_DIM**-0.5
    for i in range(blocks):
        places = [(j, j ^ key) for j in key_blocks(i, rows)]
        at = pl.ds(pl.multiple_of((i ^ key) * rows, rows), rows)
        fill_bias(bias_ref, segc_ref[at, 0:1], segr_ref, i, places)
        spots = [pl.ds(pl.multiple_of(p * rows, rows), rows) for _, p in places]

        @pl.loop(0, GROUP // 128)
        def _(pair, at=at, spots=spots):
            lanes = pl.ds(pl.multiple_of(pair * 128, 128), 128)
            first = pl.program_id(0) * (GROUP // HEAD_DIM)
            query, grad = q_ref[at, lanes], dm_ref[at, lanes]
            logs = lse_ref[at, :]
            outs = []
            for h in range(2):
                mine = (head_lane < HEAD_DIM) if h == 0 else (head_lane >= HEAD_DIM)
                qm = jnp.where(mine, query, 0) * jnp.asarray(scale, BF16)
                gm = jnp.where(mine, grad, 0)
                log = jnp.sum(
                    jnp.where(head_lane == first + pair * 2 + h, logs, 0.0), axis=1, keepdims=True
                )
                weights = [
                    jnp.exp(dot_nt(qm, k_ref[s, lanes]) + bias_ref[n] - log)
                    for n, s in enumerate(spots)
                ]
                grads = [dot_nt(gm, v_ref[s, lanes]) for s in spots]
                inner = sum(
                    jnp.sum(w * g, axis=1, keepdims=True) for w, g in zip(weights, grads)
                )
                dq = jnp.zeros((rows, 128), F32)
                for w, g, s in zip(weights, grads, spots):
                    ds = (w * (g - inner)).astype(BF16)
                    dva_ref[s, lanes] += dot_tn(w.astype(BF16), gm)
                    dka_ref[s, lanes] += dot_tn(ds, qm)
                    dq = dq + dot_nn(ds, k_ref[s, lanes])
                outs.append(dq)
            dqa_ref[at, lanes] = jnp.where(head_lane < HEAD_DIM, outs[0], outs[1]) * scale

    @pl.loop(0, blocks)
    def _(b):
        at = pl.ds(pl.multiple_of(b * rows, rows), rows)
        cosine, sine = cos_ref[at, :], sin_ref[at, :]
        dq = dqa_ref[at, :]
        dq_ref[at, :] = (dq * cosine - swap_halves(dq) * sine).astype(BF16)
        dk = dka_ref[at, :]
        dk_ref[at, :] = (dk * cosine - swap_halves(dk) * sine).astype(BF16)
        dv_ref[at, :] = dva_ref[at, :].astype(BF16)


def attn_backward(blocks, key, g, own, sib, q, k, v, lse, cosine, sine, segc, segr):
    d = g.shape[1]
    cols = q.shape[1]
    steps = cols // GROUP
    rows = LEN // blocks

    def whole(shape):
        return pl.BlockSpec(shape, lambda i: (0,) * len(shape))

    col_block = pl.BlockSpec((LEN, GROUP), lambda i: (0, i))
    weight = pl.BlockSpec((d // 2, GROUP), lambda i: (0, i))
    slab = jax.ShapeDtypeStruct((LEN, cols), BF16)
    return pl.pallas_call(
        functools.partial(attn_backward_kernel, blocks),
        grid=(steps,),
        in_specs=[pl.BlockSpec(memory_space=pltpu.SMEM), whole((LEN, d)), weight, weight]
        + [col_block] * 3
        + [whole((LEN, 128))]
        + [whole((LEN, GROUP))] * 2
        + [whole((LEN, 128)), whole(segr.shape)],
        out_specs=[col_block] * 3,
        out_shape=[slab] * 3,
        scratch_shapes=[
            pltpu.VMEM((LEN, GROUP), BF16),
            pltpu.VMEM((LEN, GROUP), F32),
            pltpu.VMEM((LEN, GROUP), F32),
            pltpu.VMEM((LEN, GROUP), F32),
            pltpu.VMEM((blocks, rows, rows), F32),
        ],
        compiler_params=pltpu.CompilerParams(vmem_limit_bytes=VMEM_BYTES),
        name="attn_backward",
    )(key, g, own, sib, q, k, v, lse, cosine, sine, segc, segr)


class LineGather:
    def __init__(self, me, src, full, sems):
        self.me, self.src, self.full, self.sems = me, src, full, sems
        self.rows = src.shape[0]

    def spot(self, side, s):
        return self.full.at[side, pl.ds(pl.multiple_of(s * self.rows, self.rows), self.rows)]

    def to_line(self, src, s, way):
        device = self.me.up if way == 0 else self.me.down
        return remote(src, self.spot(0, s), self.sems.at[way, s], self.sems.at[3, s], device)

    def to_core(self, src, s):
        return remote(src, self.spot(1, s), self.sems.at[2, s], self.sems.at[4, s], self.me.other)

    def keep(self):
        return pltpu.make_async_copy(self.src, self.spot(0, self.me.z), self.sems.at[5, 0])

    def start(self):
        z, line = self.me.z, self.me.line

        @pl.when(z + 1 < line)
        def _():
            self.to_line(self.src, z, 0).start()

        @pl.when(z >= 1)
        def _():
            self.to_line(self.src, z, 1).start()

        self.to_core(self.src, z).start()
        self.keep().start()

    def hop(self, h):
        z, line = self.me.z, self.me.line
        for s, arrives, goes_on, way in (
            (z - h, z >= h, z + 1 < line, 0),
            (z + h, z + h < line, z >= 1, 1),
        ):

            @pl.when(arrives)
            def _(s=s, goes_on=goes_on, way=way):
                here = self.spot(0, s)
                self.to_line(here, s, way).wait_recv()

                @pl.when(goes_on)
                def _():
                    self.to_line(here, s, way).start()

                self.to_core(here, s).start()

    def arrived(self):
        self.keep().wait()
        for s in range(self.me.line):
            self.to_core(self.spot(0, s), s).wait_recv()

    def done(self):
        z, line = self.me.z, self.me.line
        for s in range(line):
            here = self.spot(0, s)
            self.to_core(here, s).wait_send()

            @pl.when((s <= z) & (z + 1 < line))
            def _(s=s, here=here):
                self.to_line(here, s, 0).wait_send()

            @pl.when((s >= z) & (z >= 1))
            def _(s=s, here=here):
                self.to_line(here, s, 1).wait_send()


class SquareGather:
    def __init__(self, me, full, sems):
        self.me, self.full, self.sems = me, full, sems
        self.rows = full.shape[0] // 4

    def copies(self):
        me, full, sems, rows = self.me, self.full, self.sems, self.rows
        half = rows // 2

        def part(first, size):
            return full.at[pl.ds(first, size)]

        return (
            remote(part(0, rows), part(rows, rows), sems.at[0], sems.at[1], me.x),
            remote(part(0, rows), part(2 * rows, rows), sems.at[2], sems.at[3], me.y),
            remote(part(rows, half), part(3 * rows, half), sems.at[4], sems.at[5], me.y),
            remote(
                part(2 * rows + half, half), part(3 * rows + half, half), sems.at[6], sems.at[7], me.x
            ),
        )

    def start(self):
        x, y, _, _ = self.copies()
        x.start()
        y.start()

    def forward(self):
        x, y, top, bottom = self.copies()
        x.wait_recv()
        top.start()
        y.wait_recv()
        bottom.start()

    def arrived(self):
        _, _, top, bottom = self.copies()
        top.wait_recv()
        bottom.wait_recv()

    def done(self):
        for copy in self.copies():
            copy.wait_send()


class SquareScatter:
    def __init__(self, me, stage, landed, sems):
        self.me, self.stage, self.landed, self.sems = me, stage, landed, sems
        self.half = stage.shape[1] // 2
        self.top, self.bottom = pl.ds(0, self.half), pl.ds(self.half, self.half)

    def copies(self):
        me, stage, landed, sems = self.me, self.stage, self.landed, self.sems
        top, bottom = self.top, self.bottom
        return (
            remote(stage.at[2, top], landed.at[2, top], sems.at[0], sems.at[1], me.y),
            remote(stage.at[2, bottom], landed.at[2, bottom], sems.at[2], sems.at[3], me.x),
            remote(stage.at[0, bottom], landed.at[0, bottom], sems.at[4], sems.at[5], me.x),
            remote(stage.at[1, top], landed.at[1, top], sems.at[6], sems.at[7], me.y),
            remote(stage.at[0, top], landed.at[0, top], sems.at[8], sems.at[9], me.x),
            remote(stage.at[1, bottom], landed.at[1, bottom], sems.at[10], sems.at[11], me.y),
        )

    def diagonal_ready(self):
        copies = self.copies()
        copies[0].start()
        copies[1].start()

    def sides_ready(self):
        copies = self.copies()
        copies[2].start()
        copies[3].start()

    def combine(self):
        copies = self.copies()
        for n, slot, at in ((0, 0, self.top), (1, 1, self.bottom)):
            copies[n].wait_recv()
            add_rows(self.stage, slot, at, self.landed)
            copies[4 + n].start()

    def arrived(self):
        for copy in self.copies()[2:]:
            copy.wait_recv()

    def done(self):
        for copy in self.copies():
            copy.wait_send()


def add_rows(stage, slot, at, landed):
    step = 32

    @pl.loop(0, at.size // step)
    def _(n):
        here = pl.ds(pl.multiple_of(at.start + n * step, step), step)
        total = stage[slot, here, :].astype(F32) + landed[2, here, :].astype(F32)
        stage[slot, here, :] = total.astype(BF16)


def remote(src, dst, send_sem, recv_sem, device):
    return pltpu.make_async_remote_copy(
        src_ref=src, dst_ref=dst, send_sem=send_sem, recv_sem=recv_sem, device_id=device,
        device_id_type=pl.DeviceIdType.MESH,
    )


class Place:
    def __init__(self, dp):
        index = lax.axis_index("dp")
        self.index, self.dp = index, dp
        self.line = dp // 2
        self.z, self.core = index // 2, index % 2
        self.at_end = (self.z == 0) | (self.z == self.line - 1)
        self.t = lax.axis_index("tensor")
        tx, ty = self.t % 2, self.t // 2
        self.other = {"dp": index + 1 - 2 * self.core}
        self.up, self.down = {"dp": index + 2}, {"dp": index - 2}
        self.next, self.far = {"dp": index + 2 - 4 * (self.z % 2)}, {"dp": index + 4 - 8 * (self.z // 2)}
        self.x = {"tensor": self.t + 1 - 2 * tx}
        self.y = {"tensor": self.t + 2 - 4 * ty}
        self.spots = [
            (tx if i % 2 == 0 else 1 - tx) + 2 * (ty if i // 2 == 0 else 1 - ty) for i in range(4)
        ]

    def window(self, i, rows, seg_col, seg_ref, bias_ref):
        spots = []
        for n in range(-(-(MOST - 1) // rows) + 1):
            j = jnp.maximum(i - n, 0)
            place = (j % 2 + self.t % 2) % 2 + 2 * ((j // 2 + self.t // 2) % 2)
            same = seg_col == seg_ref[place][0:1, :]
            if n == 0:
                row = lax.broadcasted_iota(jnp.int32, (rows, rows), 0)
                col = lax.broadcasted_iota(jnp.int32, (rows, rows), 1)
                bias_ref[n] = jnp.where(same & (col <= row), 0.0, NEG)
            else:
                bias_ref[n] = jnp.where(same, jnp.where(i >= n, 0.0, NEG), NEG)
            spots.append(pl.ds(pl.multiple_of(place * rows, rows), rows))
        return spots

    def greet(self):
        barrier = pltpu.get_barrier_semaphore()
        peers = [self.x, self.y] + [{"dp": (self.index + k) % self.dp} for k in range(1, self.dp)]
        for device in peers:
            pl.semaphore_signal(
                barrier, inc=1, device_id=device, device_id_type=pl.DeviceIdType.MESH
            )
        pl.semaphore_wait(barrier, len(peers))


def norm_rows(count, body, step=32):
    @pl.loop(0, count // step)
    def _(n):
        body(pl.ds(pl.multiple_of(n * step, step), step))


def attend(pair, first, at, spots, head_lane, q_ref, k_ref, v_ref, mixed_ref, lse_ref, bias_ref):
    lanes = pl.ds(pl.multiple_of(pair * 128, 128), 128)
    query = q_ref[at, lanes]
    outs, stats = [], []
    for h in range(2):
        mine = (head_lane < HEAD_DIM) if h == 0 else (head_lane >= HEAD_DIM)
        qm = jnp.where(mine, query, 0) * jnp.asarray(HEAD_DIM**-0.5, BF16)
        scores = [dot_nt(qm, k_ref[s, lanes]) + bias_ref[n] for n, s in enumerate(spots)]
        top = functools.reduce(jnp.maximum, [jnp.max(s, axis=1, keepdims=True) for s in scores])
        weights = [jnp.exp(s - top) for s in scores]
        total = sum(jnp.sum(w, axis=1, keepdims=True) for w in weights)
        out = sum(dot_nn(w.astype(BF16), v_ref[s, lanes]) for w, s in zip(weights, spots))
        outs.append(out / total)
        stats.append(top + jnp.log(total))
    mixed_ref[at, lanes] = jnp.where(head_lane < HEAD_DIM, outs[0], outs[1]).astype(BF16)
    kept = jnp.where(pair + first == 0, 0.0, lse_ref[at, :])
    for h in range(2):
        kept = jnp.where(head_lane == first + pair * 2 + h, stats[h], kept)
    lse_ref[at, :] = kept


def add_into(total, other, rows, step=64):
    @pl.loop(0, rows // step)
    def _(n):
        at = pl.ds(pl.multiple_of(n * step, step), step)
        total[at, :] = (total[at, :].astype(F32) + other[at, :].astype(F32)).astype(total.dtype)


KEPT_SLOT = 6


class LineScatter:
    def __init__(self, me, rows, mine, theirs, swapped, kept, landed, work, sems, step_sems):
        cut = lambda ref: ref.at[:, pl.ds(0, rows)]
        self.me, self.rows = me, rows
        self.mine, self.theirs, self.swapped = cut(mine), cut(theirs), cut(swapped)
        self.kept, self.landed, self.work = cut(kept), cut(landed), cut(work)
        self.sems, self.step_sems = sems, step_sems

    def swap(self):
        return remote(
            self.theirs, self.swapped, self.step_sems.at[0], self.step_sems.at[1], self.me.other
        )

    def keep(self):
        return pltpu.make_async_copy(self.mine, self.kept, self.step_sems.at[2])

    def send(self, src, s, upward, z):
        line = self.me.line
        if upward:
            slot, device = s, self.me.up
        else:
            slot, device = (s if s < z - 1 else line), self.me.down
        return remote(
            src, self.landed.at[slot], self.sems.at[s], self.sems.at[line + slot], device
        )

    def landing(self, slot):
        line = self.me.line
        return remote(
            self.landed.at[slot], self.landed.at[slot], self.sems.at[0],
            self.sems.at[line + slot], self.me.other,
        )

    def load(self, src, n):
        return pltpu.make_async_copy(src, self.work.at[n], self.step_sems.at[3 + n])

    def reduce(self, free_sem):
        line = self.me.line
        self.swap().wait_recv()
        for s in range(line):
            add_into(self.mine.at[s], self.swapped.at[s], self.rows)
        pl.semaphore_signal(
            free_sem, inc=1, device_id=self.me.other, device_id_type=pl.DeviceIdType.MESH
        )
        self.keep().start()
        self.swap().wait_send()
        self.keep().wait()
        for end, upward in ((0, True), (line - 1, False)):

            @pl.when(self.me.z == end)
            def _(end=end, upward=upward):
                order = range(line - 1, end, -1) if upward else range(end)
                for s in order:
                    self.send(self.kept.at[s], s, upward, end).start()

    def going(self, p):
        line = self.me.line
        for z, upward in ((p, True), (line - 1 - p, False)):
            targets = list(range(line - 1, z, -1)) if upward else list(range(z))
            yield z, upward, targets

    def run_phase(self, p, first):
        for z, upward, targets in self.going(p):

            @pl.when(self.me.z == z)
            def _(z=z, upward=upward, targets=targets):
                for n, s in enumerate(targets):
                    self.load(self.kept.at[s], KEPT_SLOT + n).start()
                for n, s in enumerate(targets):
                    a, b = first + n, KEPT_SLOT + n
                    self.landing(s).wait_recv()
                    self.load(self.landed.at[s], a).start()
                    self.load(self.kept.at[s], b).wait()
                    self.load(self.landed.at[s], a).wait()
                    add_into(self.work.at[a], self.work.at[b], self.rows)
                    self.send(self.work.at[a], s, upward, z).start()

    def sent_phase(self, p, first):
        for z, upward, targets in self.going(p):

            @pl.when(self.me.z == z)
            def _(z=z, upward=upward, targets=targets):
                for n, s in enumerate(targets):
                    self.send(self.work.at[first + n], s, upward, z).wait_send()

    def load_last(self, first):
        me = self.me
        self.load(self.kept.at[me.z], first).start()

        @pl.when(me.z >= 1)
        def _():
            self.landing(me.z).wait_recv()
            self.load(self.landed.at[me.z], first + 1).start()

        @pl.when(me.z < me.line - 1)
        def _():
            self.landing(me.line).wait_recv()
            self.load(self.landed.at[me.line], first + 2).start()

    def run_last(self, first, total):
        me = self.me
        here = total.at[pl.ds(0, self.rows)]
        self.load(self.kept.at[me.z], first).wait()

        def put(n, step=64):
            @pl.loop(0, self.rows // step)
            def _(i):
                at = pl.ds(pl.multiple_of(i * step, step), step)
                if n == first:
                    here[at, :] = self.work[n, at, :].astype(F32)
                else:
                    here[at, :] += self.work[n, at, :].astype(F32)

        put(first)

        @pl.when(me.z >= 1)
        def _():
            self.load(self.landed.at[me.z], first + 1).wait()
            put(first + 1)

        @pl.when(me.z < me.line - 1)
        def _():
            self.load(self.landed.at[me.line], first + 2).wait()
            put(first + 2)

    def done(self):
        line = self.me.line
        for end, upward in ((0, True), (line - 1, False)):

            @pl.when(self.me.z == end)
            def _(end=end, upward=upward):
                for s in range(line - 1, end, -1) if upward else range(end):
                    self.send(self.kept.at[s], s, upward, end).wait_send()


WORK_SLOTS = (0, 2, 4, 5)


class Ticks:
    def __init__(self, chunks, total, writers, held):
        self.chunks, self.total, self.writers, self.held = chunks, total, writers, held
        self.k, self.second, self.last, self.written = 0, 0, 0, 0
        self.sent = [None] * len(WORK_SLOTS)

    def run(self, chunk, p, group):
        first = WORK_SLOTS[group]
        if self.sent[group] is not None:
            self.sent[group].sent_phase(p, first)
        chunk.run_phase(p, first)
        self.sent[group] = chunk

    def finish(self, n):
        self.chunks[n].load_last(KEPT_SLOT)
        if n > 0:
            self.writers[n - 1].wait()
        self.chunks[n].run_last(KEPT_SLOT, self.total)
        self.writers[n].start()

    def tick(self, most=2, last=2):
        k, count = self.k, len(self.chunks)
        ready, done = min(k, count), self.second
        if k >= self.held:
            for _ in range(most):
                if self.second < ready:
                    self.run(self.chunks[self.second], 2, 2 + self.second % 2)
                    self.second += 1
        if k < count:
            self.run(self.chunks[k], 1, k % 2)
        if k >= self.held:
            for _ in range(last):
                if self.last < done:
                    self.finish(self.last)
                    self.last += 1
        self.k += 1

    def rest(self):
        while self.last < len(self.chunks):
            self.tick(3, 3)

    def done(self):
        self.writers[-1].wait()
        for group, p in ((0, 1), (1, 1), (2, 2), (3, 2)):
            self.sent[group].sent_phase(p, WORK_SLOTS[group])
        for chunk in self.chunks:
            chunk.done()


class Writer:
    def __init__(self, total, turned, parts, sem):
        self.total, self.turned, self.parts, self.sem = total, turned, parts, sem

    def copies(self):
        for n, (dst, _) in enumerate(self.parts):
            yield pltpu.make_async_copy(self.turned.at[n], dst, self.sem.at[n])

    def start(self):
        for n, (_, flip) in enumerate(self.parts):
            block = self.total[pl.ds(n * 256, 256), :]
            self.turned[n] = (block.T if flip else block).astype(BF16)
        for copy in self.copies():
            copy.start()

    def wait(self):
        for copy in self.copies():
            copy.wait()


def norm_back_rows(count, gain, values_of, grads_of, gain_ref, row, put, step=32):
    @pl.loop(0, count // step)
    def _(n):
        at = pl.ds(pl.multiple_of(n * step, step), step)
        values, grads = values_of(at), grads_of(at)
        factor = norm_factor(values)
        scaled = grads * gain
        back = factor * scaled - values * factor * factor * factor * jnp.mean(
            scaled * values, axis=-1, keepdims=True
        )
        gain_ref[row : row + 1, :] += jnp.sum(grads * values * factor, axis=0, keepdims=True)
        put(at, back)


def attend_back(
    pair, at, spots, head_lane, q_ref, k_ref, v_ref, dm_ref, lse_ref, bias_ref, dqa_ref, dka_ref, dva_ref
):
    scale = HEAD_DIM**-0.5
    rows = at.size
    lanes = pl.ds(pl.multiple_of(pair * 128, 128), 128)
    query, grad = q_ref[at, lanes], dm_ref[at, lanes]
    logs = lse_ref[at, :]
    outs = []
    for h in range(2):
        mine = (head_lane < HEAD_DIM) if h == 0 else (head_lane >= HEAD_DIM)
        qm = jnp.where(mine, query, 0) * jnp.asarray(scale, BF16)
        gm = jnp.where(mine, grad, 0)
        log = jnp.sum(
            jnp.where(head_lane == pair * 2 + h, logs, 0.0), axis=1, keepdims=True
        )
        weights = [
            jnp.exp(dot_nt(qm, k_ref[s, lanes]) + bias_ref[n] - log) for n, s in enumerate(spots)
        ]
        grads = [dot_nt(gm, v_ref[s, lanes]) for s in spots]
        inner = sum(jnp.sum(w * g, axis=1, keepdims=True) for w, g in zip(weights, grads))
        dq = jnp.zeros((rows, 128), F32)
        for w, g, s in zip(weights, grads, spots):
            ds = (w * (g - inner)).astype(BF16)
            dva_ref[s, lanes] += dot_tn(w.astype(BF16), gm)
            dka_ref[s, lanes] += dot_tn(ds, qm)
            dq = dq + dot_nn(ds, k_ref[s, lanes])
        outs.append(dq)
    dqa_ref[:, lanes] = jnp.where(head_lane < HEAD_DIM, outs[0], outs[1]) * scale


TICK_AFTER = (3, 5, 6)
TICK_HELD = 3


def layer_kernel(
    dp, x_in, g_in, gain_ref, wq_in, wk_in, wv_in, wo_in, gate_in, up_in, down_in, doc_ref,
    output_out, input_grad_out, gain_out, gate_out, up_out, down_out, q_out, k_out, v_out, o_out,
    wa_full, wo_full, wf_full, hidden_all, kept_all, landed_all, y_all, normed_all, q_all, k_all, v_all,
    mixed_all, lse_all, cos_all, sin_all, segc_all, segr_all,
    x_ref, wa_src, wo_src, wf_src, gains_full, rows_a, rows_m, rows_g,
    theirs, swapped, mine, work, total, turned, stage, landed, own, gm, middle, gp, gp_landed,
    sem_in, sem_gains, sem_a, sem_o, sem_f, sem_n, sem_m, sem_g, sem_g2, sem_s, sem_line, sem_step, sem_write,
    sem_gain, sem_c, sem_w, free_core, free_x, free_y,
):
    me = Place(dp)
    line = me.line
    d = x_in.shape[1]
    half, local = d // 2, x_in.shape[0]
    shard = half // line
    rows = LEN // 4
    blocks = wf_src.shape[0]
    fw = wf_src.shape[2] // 3
    cols = wq_in.shape[1]
    groups = cols // GROUP

    def at_block(b):
        return pl.ds(pl.multiple_of(b * rows, rows), rows)

    def true_columns(side, s):
        core = me.core if side == 0 else 1 - me.core
        return pl.ds(pl.multiple_of((2 * s + core) * shard, shard), shard)

    def own_columns(side, s):
        return pl.ds(side * half + s * shard, shard)

    sides = [(side, s) for side in range(2) for s in range(line)]
    x_loads = [
        pltpu.make_async_copy(
            x_in.at[:, true_columns(*p)], x_ref.at[:, own_columns(*p)], sem_in.at[n]
        )
        for n, p in enumerate(sides)
    ]
    g_loads = [
        pltpu.make_async_copy(
            g_in.at[:, true_columns(*p)], rows_g.at[pl.ds(0, local), own_columns(*p)],
            sem_in.at[2 * line + n],
        )
        for n, p in enumerate(sides)
    ]
    first_sem = 4 * line
    a_loads = [
        pltpu.make_async_copy(ref, wa_src.at[:, pl.ds(n * cols, cols)], sem_in.at[first_sem + n])
        for n, ref in enumerate((wq_in, wk_in, wv_in))
    ]
    f_loads = [
        pltpu.make_async_copy(
            ref.at[:, pl.ds(n * fw, fw)], wf_src.at[n, :, pl.ds(part * fw, fw)],
            sem_in.at[first_sem + 3 + 2 * n + part],
        )
        for n in range(blocks)
        for part, ref in enumerate((gate_in, up_in))
    ]
    for copy in a_loads + x_loads + g_loads + f_loads:
        copy.start()
    gains_full[0, pl.ds(pl.multiple_of(me.z * 16, 16), 16), :] = gain_ref[...]
    me.greet()

    def gain_copy(k, sender):
        place = gains_full.at[k % 2, pl.ds(pl.multiple_of(sender // 2 * 16, 16), 16)]
        return remote(
            gain_ref, place, sem_gains.at[0, k], sem_gains.at[1, k], {"dp": (me.index + k) % dp}
        )

    for k in range(1, dp):
        gain_copy(k, me.index).start()

    wa = LineGather(me, wa_src, wa_full, sem_a)
    wo = LineGather(me, wo_src, wo_full, sem_o)
    gathers = [LineGather(me, wf_src.at[n], wf_full.at[n], sem_f.at[n]) for n in range(blocks)]
    order = [wa, wo] + gathers

    def start_all():
        for one in gathers:
            one.start()

    acts = []
    for n, one in enumerate(order):
        for h in range(1, line):

            def act(n=n, one=one, h=h):
                one.hop(h)
                if h == 2 and n == 0:
                    wo.start()
                    pl.when(me.at_end)(start_all)
                if n == 1 and h == 2:
                    pl.when(jnp.logical_not(me.at_end))(gathers[0].start)
                    pl.when(jnp.logical_not(me.at_end))(gathers[1].start)
                if h == 1 and 2 <= n < blocks:
                    pl.when(jnp.logical_not(me.at_end))(order[n + 2].start)

            acts.append(act)

    def poll(count=1):
        for _ in range(min(count, len(acts))):
            acts.pop(0)()

    def hops_done(n):
        return len(acts) <= (blocks - 1 - n) * (line - 1)

    for copy in a_loads:
        copy.wait()
    wa.start()
    for k in range(1, dp):
        gain_copy(k, (me.index + dp - k) % dp).wait_recv()
    for copy in x_loads:
        copy.wait()

    def gain_row(which):
        return jnp.concatenate(
            [
                gains_full[side, pl.ds(s * 16 + which, 1), :].astype(F32)
                for side in range(2)
                for s in range(line)
            ],
            axis=1,
        )

    gain_one, gain_two = gain_row(0), gain_row(1)

    def first_norm(at):
        values = x_ref[at, :].astype(F32)
        rows_a[at, :] = (values * norm_factor(values) * gain_one).astype(BF16)

    norm_rows(local, first_norm)
    normed = SquareGather(me, rows_a, sem_n)
    grads = SquareGather(me, rows_g, sem_g)
    normed_mlp = SquareGather(me, rows_m, sem_m)
    square = SquareGather(me, rows_a, sem_g2)
    scatter = SquareScatter(me, stage, landed, sem_s)
    normed.start()
    for n in range(cols // 256):
        wo_src[:, pl.ds(n * 256, 256)] = wo_in[pl.ds(n * 256, 256), :].T
    for n in range(blocks):
        wf_src[n, :, pl.ds(2 * fw, fw)] = down_in[pl.ds(n * fw, fw), :].T

    def tables(cos_ref, sin_ref, segc_ref, segr_ref):
        ends = []
        for k in range(doc_ref.shape[1]):
            length = doc_ref[0:1, k : k + 1]
            ends.append((length, length + ends[-1][1] if ends else length))

        def place_of(token):
            segment, first = jnp.zeros_like(token), jnp.zeros_like(token)
            for length, end in ends:
                passed = token >= end
                segment = segment + jnp.where(passed, 1, 0)
                first = first + jnp.where(passed, length, 0)
            return segment, token - first

        lane = lax.broadcasted_iota(jnp.int32, (1, 128), 1)
        pair = (lane % (HEAD_DIM // 2)).astype(F32)
        inverse = jnp.exp(pair * (-2.0 / HEAD_DIM * math.log(ROPE_BASE)))
        sign = jnp.where(lane % HEAD_DIM < HEAD_DIM // 2, -1.0, 1.0)
        for p in range(4):
            at = pl.ds(p * rows, rows)
            begin = me.spots[p] * rows
            segment, position = place_of(begin + lax.broadcasted_iota(jnp.int32, (rows, 128), 0))
            segc_ref[at, :] = segment
            angle = position.astype(F32) * inverse
            cos_ref[at, :] = jnp.cos(angle)
            sin_ref[at, :] = jnp.sin(angle) * sign
            segr_ref[p] = place_of(begin + lax.broadcasted_iota(jnp.int32, (8, rows), 1))[0]
        out = [
            pltpu.make_async_copy(a, b, sem_c.at[n])
            for n, (a, b) in enumerate(
                ((cos_ref, cos_all), (sin_ref, sin_all), (segc_ref, segc_all), (segr_ref, segr_all))
            )
        ]
        for copy in out:
            copy.start()
        for copy in out:
            copy.wait()

    table = pltpu.VMEM((LEN, 128), F32)
    segs = (pltpu.VMEM(segc_all.shape, jnp.int32), pltpu.VMEM(segr_all.shape, jnp.int32))
    pl.run_scoped(tables, table, table, *segs)
    for copy in f_loads:
        copy.wait()
    poll()
    for copy in g_loads:
        copy.wait()
    normed.forward()
    grads.start()
    poll(line - 2)
    normed.arrived()
    wa.arrived()

    def free_landed():
        for device, sem in ((me.x, free_x), (me.y, free_y)):
            pl.semaphore_signal(
                sem, inc=1, device_id=device, device_id_type=pl.DeviceIdType.MESH
            )

    def wait_free():
        pl.semaphore_wait(free_x, 1)
        pl.semaphore_wait(free_y, 1)

    def summed(at):
        return own[at, :] + landed[0, at, :].astype(F32) + landed[1, at, :].astype(F32)

    def doubled(ref, at):
        part = ref[at, :]
        return jnp.concatenate([part] * (GROUP // 128), axis=1)

    head_lane = lax.broadcasted_iota(jnp.int32, (rows, 128), 1)

    def forward(
        wa_v, wo_v, q_ref, k_ref, v_ref, mixed_ref, mixed_t, lse_ref, cos_ref, sin_ref, segc_ref, segr_ref, bias_ref
    ):
        ins = [(cos_all, cos_ref), (sin_all, sin_ref), (segc_all, segc_ref), (segr_all, segr_ref)] + [
            (wa_full.at[side], wa_v.at[pl.ds(side * half, half)]) for side in range(2)
        ]
        loads = [pltpu.make_async_copy(a, b, sem_c.at[n]) for n, (a, b) in enumerate(ins)]
        for copy in loads:
            copy.start()
        for copy in loads:
            copy.wait()

        @pl.loop(0, 2)
        def _(r):
            at = pl.ds(pl.multiple_of(r * 2 * rows, 2 * rows), 2 * rows)
            cosine = jnp.concatenate([cos_ref[at, :]] * (cols // 128), axis=1)
            sine = jnp.concatenate([sin_ref[at, :]] * (cols // 128), axis=1)

            def product(part):
                return dot_nn(rows_a[at, :], wa_v[:, pl.ds(part * cols, cols)])

            query = product(0)
            q_ref[at, :] = (query * cosine + swap_halves(query) * sine).astype(BF16)
            keys = product(1)
            k_ref[at, :] = (keys * cosine + swap_halves(keys) * sine).astype(BF16)
            v_ref[at, :] = product(2).astype(BF16)

        outs = [(q_ref, q_all), (k_ref, k_all), (v_ref, v_all), (rows_a, normed_all)]
        stores = [pltpu.make_async_copy(a, b, sem_c.at[n]) for n, (a, b) in enumerate(outs)]
        for copy in stores:
            copy.start()
        poll(2)
        for i in range(4):
            places = [(j, me.spots[j]) for j in key_blocks(i, rows)]
            at = at_block(me.spots[i])
            fill_bias(bias_ref, segc_ref[at, 0:1], segr_ref, i, places)
            spots = [at_block(p) for _, p in places]

            @pl.loop(0, cols // 128)
            def _(pair, at=at, spots=spots):
                attend(pair, 0, at, spots, head_lane, q_ref, k_ref, v_ref, mixed_ref, lse_ref, bias_ref)

            if i == 0:
                poll(line - 3)
            if i == 1:
                grads.forward()
            if i == 2:
                wo.arrived()
                wo_load = [
                    pltpu.make_async_copy(wo_full.at[side], wo_v.at[pl.ds(side * half, half)], sem_w.at[0, side])
                    for side in range(2)
                ]
                for copy in wo_load:
                    copy.start()
                poll()
        mixed_t[...] = mixed_ref[...].T
        for n, (a, b) in enumerate(((mixed_t, mixed_all), (lse_ref, lse_all))):
            stores.append(pltpu.make_async_copy(a, b, sem_c.at[len(outs) + n]))
            stores[-1].start()
        for copy in wo_load:
            copy.wait()

        def out_rows(b, slot, count=1):
            at = pl.ds(b * rows, count * rows)
            for side in range(2):
                here = pl.ds(side * half, half)
                value = dot_nt(mixed_ref[at, :], wo_v[here, :])
                if slot is None:
                    own[:, here] = value
                else:
                    for k in range(count):
                        stage[slot + k, :, here] = value[k * rows : (k + 1) * rows].astype(BF16)

        out_rows(3, 2)
        scatter.diagonal_ready()
        out_rows(1, 0, 2)
        scatter.sides_ready()
        out_rows(0, None)
        poll()
        scatter.combine()
        poll(3)
        for copy in stores:
            copy.wait()
        normed.done()
        scatter.arrived()

    V = pltpu.VMEM
    slab = V((LEN, cols), BF16)
    bias = V((3, rows, rows), F32)
    pl.run_scoped(
        forward, V((d, 3 * cols), BF16), V((d, cols), BF16), slab, slab, slab, slab, V((cols, LEN), BF16), table, table, table,
        *segs, bias,
    )

    def second_norm(at):
        values = x_ref[at, :].astype(F32) + summed(at)
        middle[at, :] = values
        rows_m[at, :] = (values * norm_factor(values) * gain_two).astype(BF16)

    norm_rows(local, second_norm)
    normed_mlp.start()
    free_landed()
    scatter.done()
    poll(2)
    grads.arrived()

    sizes = [3 * fw] * blocks + [cols] + [3 * GROUP] * groups
    chunks = [
        LineScatter(me, size, mine, theirs, swapped, kept_all.at[n], landed_all.at[n], work, sem_line.at[n], sem_step)
        for n, size in enumerate(sizes)
    ]
    writers = []
    for n in range(blocks):
        here = pl.ds(n * fw, fw)
        parts = [(gate_out.at[:, here], True), (up_out.at[:, here], True), (down_out.at[here], False)]
        writers.append(Writer(total, turned, parts, sem_write))
    parts = [(o_out.at[pl.ds(n * 256, 256)], False) for n in range(cols // 256)]
    writers.append(Writer(total, turned, parts, sem_write))
    for n in range(groups):
        here = pl.ds(n * GROUP, GROUP)
        parts = [(ref.at[:, here], True) for ref in (q_out, k_out, v_out)]
        writers.append(Writer(total, turned, parts, sem_write))
    ticks = Ticks(chunks, total, writers, TICK_HELD)

    def swap(n):
        if n >= 1:
            pl.semaphore_wait(free_core, 1)
        chunks[n].swap().start()

    def products(left, right, first, size):
        for side, dst in ((0, mine), (1, theirs)):
            value = dot_nn(left[...], right[:, pl.ds(side * half, half)]).astype(BF16)
            for s in range(line):
                dst[s, pl.ds(first, size), :] = value[:, s * shard : (s + 1) * shard]

    def mlp(wb, sums, dgu_t, hid_t, hid):
        def weights(n):
            return [
                pltpu.make_async_copy(
                    wf_full.at[n, side], wb.at[n % 2, pl.ds(side * half, half)], sem_w.at[n % 2, side]
                )
                for side in range(2)
            ]

        def hidden_copy(n):
            return pltpu.make_async_copy(hid.at[n % 2], hidden_all.at[n], sem_c.at[n % 2])

        fetched = [False] * (blocks + 1)

        def to_stage(b, slot):
            @pl.loop(0, rows // 64)
            def _(i):
                at = pl.ds(pl.multiple_of(i * 64, 64), 64)
                there = pl.ds(pl.multiple_of(b * rows + i * 64, 64), 64)
                if slot is None:
                    own[at, :] = sums[there, :]
                else:
                    stage[slot, at, :] = sums[there, :].astype(BF16)

        def fetch(n):
            if n < blocks and not fetched[n]:
                while not hops_done(n):
                    poll()
                gathers[n].arrived()
                for copy in weights(n):
                    copy.start()
                fetched[n] = True

        for n in range(blocks):
            fetch(n)
            if n == 0:

                @pl.loop(0, LEN // 64)
                def _(i):
                    at = pl.ds(pl.multiple_of(i * 64, 64), 64)
                    sums[at, :] = jnp.zeros((64, d), F32)

            for copy in weights(n):
                copy.wait()
            if n == 1:
                chunks[0].reduce(free_core)
            if n + 1 < blocks and hops_done(n + 1):
                fetch(n + 1)
            if n >= 2:
                hidden_copy(n - 2).wait()
            w = wb.at[n % 2]
            gu_w, down_w = w.at[:, pl.ds(0, 2 * fw)], w.at[:, pl.ds(2 * fw, fw)]

            def block_rows(at, n=n, gu_w=gu_w, down_w=down_w):
                gu = dot_nn(rows_m[at, :], gu_w[...])
                grad_hidden = dot_nn(rows_g[at, :], down_w[...])
                gate_pre, upward = gu[:, :fw], gu[:, fw:]
                sig = jax.nn.sigmoid(gate_pre)
                activated = gate_pre * sig
                hidden = (activated * upward).astype(BF16)
                hid[n % 2, at, :] = hidden
                hid_t[:, at] = hidden.T
                grad_gate = grad_hidden * upward * sig * (1.0 + gate_pre * (1.0 - sig))
                grad_up = grad_hidden * activated
                dgu = jnp.concatenate([grad_gate, grad_up], axis=1).astype(BF16)
                dgu_t[:, at] = dgu.T

                @pl.loop(0, 2)
                def _(c):
                    here = pl.ds(pl.multiple_of(c * half, half), half)
                    sums[at, here] += dot_nt(dgu, gu_w[here, :])

            if n == 0:
                block_rows(pl.ds(0, rows))
                poll()
                normed_mlp.forward()
                block_rows(pl.ds(rows, 2 * rows))
                normed_mlp.arrived()
                block_rows(pl.ds(3 * rows, rows))
                poll()
            elif n == blocks - 1:
                wait_free()
                block_rows(pl.ds(3 * rows, rows))
                to_stage(3, 2)
                scatter.diagonal_ready()
                block_rows(pl.ds(rows, 2 * rows))
                to_stage(1, 0)
                to_stage(2, 1)
                scatter.sides_ready()
                block_rows(pl.ds(0, rows))
                to_stage(0, None)
            else:
                @pl.loop(0, 2)
                def _(r, block_rows=block_rows):
                    block_rows(pl.ds(pl.multiple_of(r * 2 * rows, 2 * rows), 2 * rows))
            hidden_copy(n).start()
            if n % 2 == 1:
                poll()
            if n >= 2:
                chunks[n - 1].reduce(free_core)
            products(dgu_t, rows_m, 0, 2 * fw)
            products(hid_t, rows_g, 2 * fw, fw)
            swap(n)
            poll()
            if n in TICK_AFTER:
                ticks.tick()
        for n in range(max(0, blocks - 2), blocks):
            hidden_copy(n).wait()

    pl.run_scoped(
        mlp, V((2, d, 3 * fw), BF16), V((LEN, d), F32), V((2 * fw, LEN), BF16), V((fw, LEN), BF16),
        V((2, LEN, fw), BF16),
    )
    gp[...] = jnp.zeros(gp.shape, F32)

    def down(hidden, dw, rest):
        ins = [(hidden_all.at[n], hidden.at[:, pl.ds(n * fw, fw)]) for n in range(blocks)] + [
            (
                wf_full.at[n, side, :, pl.ds(2 * fw, fw)],
                dw.at[pl.ds(side * half, half), pl.ds(n * fw, fw)],
            )
            for n in range(blocks)
            for side in range(2)
        ]
        loads = [pltpu.make_async_copy(a, b, sem_c.at[n]) for n, (a, b) in enumerate(ins)]
        for copy in loads:
            copy.start()
        scatter.combine()
        ticks.tick()
        for copy in loads:
            copy.wait()

        @pl.loop(0, 4)
        def _(n):
            at = pl.ds(pl.multiple_of(n // 2 * 2 * rows, 2 * rows), 2 * rows)
            here = pl.ds(pl.multiple_of(n % 2 * half, half), half)
            rest[at, here] = dot_nt(hidden[at, :], dw[here, :]).astype(BF16)

        out = pltpu.make_async_copy(rest, y_all, sem_c.at[0])
        out.start()
        out.wait()

    pl.run_scoped(
        down, V((LEN, blocks * fw), BF16), V((d, blocks * fw), BF16), V((LEN, d), BF16)
    )
    normed_mlp.done()
    grads.done()

    def attention(
        q_ref, k_ref, v_ref, mixed_t, lse_ref, cos_ref, sin_ref, segc_ref, segr_ref, out_w,
        dqa_ref, dka_ref, dva_ref, part_t, bias_ref,
    ):
        ins = [
            (q_all, q_ref), (k_all, k_ref), (v_all, v_ref), (lse_all, lse_ref), (cos_all, cos_ref),
            (sin_all, sin_ref), (segc_all, segc_ref), (segr_all, segr_ref), (wo_full, out_w),
            (mixed_all, mixed_t), (normed_all, rows_m),
        ]
        loads = [pltpu.make_async_copy(a, b, sem_c.at[n]) for n, (a, b) in enumerate(ins)]
        for copy in loads:
            copy.start()
        scatter.arrived()

        def second_norm_back(at, back):
            grad = rows_g[at, :].astype(F32) + back
            gm[at, :] = grad
            rows_a[at, :] = grad.astype(BF16)

        norm_back_rows(local, gain_two, lambda at: middle[at, :], summed, gp, 1, second_norm_back)
        square.start()
        free_landed()
        scatter.done()
        stage_in = [
            pltpu.make_async_copy(y_all.at[pl.ds(b * rows, rows)], stage.at[slot], sem_w.at[n // 2, n % 2])
            for n, (b, slot) in enumerate(((3, 2), (1, 0), (2, 1)))
        ]
        for copy in stage_in:
            copy.start()
        chunks[blocks - 1].reduce(free_core)
        ticks.tick()
        for copy in loads:
            copy.wait()

        @pl.loop(0, 4)
        def _(b):
            at = at_block(b)
            dka_ref[at, :] = jnp.zeros((rows, cols), F32)
            dva_ref[at, :] = jnp.zeros((rows, cols), F32)

        dm_ref = rows_g.at[:, pl.ds(3 * cols, cols)]

        def query_block(p, between=None):
            at = pl.ds(p * rows, rows)
            dm_ref[at, :] = (
                dot_nn(rows_a[at, :half], out_w[0]) + dot_nn(rows_a[at, half:], out_w[1])
            ).astype(BF16)
            spots = me.window(me.spots[p], rows, segc_ref[at, 0:1], segr_ref, bias_ref)

            def one_pair(pair):
                attend_back(
                    pair, at, spots, head_lane, q_ref, k_ref, v_ref, dm_ref, lse_ref, bias_ref,
                    dqa_ref, dka_ref, dva_ref,
                )

            pairs = GROUP // 128
            if between is None:
                pl.loop(0, cols // 128)(one_pair)
            for group in range(groups):
                if between is not None:
                    pl.loop(group * pairs, (group + 1) * pairs)(one_pair)
                lanes = pl.ds(group * GROUP, GROUP)
                value = dqa_ref[:, lanes]
                value = value * doubled(cos_ref, at) - swap_halves(value) * doubled(sin_ref, at)
                rows_g[at, lanes] = value.astype(BF16)
                if between is not None:
                    between(group)

        query_block(0)
        ticks.tick()
        square.forward()
        query_block(1)
        query_block(2)
        ticks.tick()
        for copy in stage_in:
            copy.wait()
        wait_free()
        square.arrived()
        scatter.diagonal_ready()
        scatter.sides_ready()
        products(mixed_t, rows_a, 0, cols)
        swap(blocks)
        def turn(group):
            @pl.loop(0, 4)
            def _(b):
                at = at_block(b)
                cosine, sine = doubled(cos_ref, at), doubled(sin_ref, at)
                for part, ref in enumerate((None, dka_ref, dva_ref)):
                    lanes = pl.ds(group * GROUP, GROUP)
                    there = pl.ds(part * cols + group * GROUP, GROUP)
                    if part == 0:
                        value = rows_g[at, there]
                    else:
                        value = ref[at, lanes]
                        if part == 1:
                            value = value * cosine - swap_halves(value) * sine
                        value = value.astype(BF16)
                        rows_g[at, there] = value
                    part_t[pl.ds(part * GROUP, GROUP), at] = value.T

        def finish_group(group):
            chunks[blocks + group].reduce(free_core)
            turn(group)
            products(part_t, rows_m, 0, 3 * GROUP)
            swap(blocks + 1 + group)
            if group == 0:
                scatter.combine()
                ticks.tick()

        query_block(3, finish_group)

    pl.run_scoped(
        attention, slab, slab, slab, V((cols, LEN), BF16), table, table, table, *segs,
        V(wo_full.shape, BF16), V((rows, cols), F32), V((LEN, cols), F32), V((LEN, cols), F32),
        V((3 * GROUP, LEN), BF16), bias,
    )

    def normed_grads(qkv_w, stage_two, y_mine):
        ins = [(wa_full.at[side], qkv_w.at[pl.ds(side * half, half)]) for side in range(2)]
        ins.append((y_all.at[pl.ds(0, rows)], y_mine))
        loads = [pltpu.make_async_copy(a, b, sem_c.at[n]) for n, (a, b) in enumerate(ins)]
        for copy in loads:
            copy.start()
        for copy in loads:
            copy.wait()

        def normed_grad(b, slot, count=1):
            at = pl.ds(b * rows, count * rows)
            for side in range(2):
                here = pl.ds(side * half, half)
                value = dot_nt(rows_g[at, pl.ds(0, 3 * cols)], qkv_w[here, :])
                if slot is None:
                    own[:, here] = value
                else:
                    for k in range(count):
                        stage_two[slot + k, :, here] = value[k * rows : (k + 1) * rows].astype(BF16)

        normed_grad(3, 2)
        normed_grad(1, 0, 2)
        normed_grad(0, None)
        scatter.arrived()

        def output_rows(at):
            value = middle[at, :] + y_mine[at, :].astype(F32)
            value = value + landed[0, at, :].astype(F32) + landed[1, at, :].astype(F32)
            y_mine[at, :] = value.astype(BF16)

        norm_rows(local, output_rows)
        free_landed()
        results = [
            pltpu.make_async_copy(
                y_mine.at[:, own_columns(*p)], output_out.at[:, true_columns(*p)], sem_in.at[n]
            )
            for n, p in enumerate(sides)
        ]
        for copy in results:
            copy.start()
        scatter.done()
        wait_free()
        scatter_two = SquareScatter(me, stage_two, landed, sem_s)
        scatter_two.diagonal_ready()
        scatter_two.sides_ready()
        chunks[blocks + groups].reduce(free_core)
        ticks.tick(2, 2)
        for copy in results:
            copy.wait()
        scatter_two.combine()
        ticks.tick(3, 2)
        ticks.tick(3, 0)
        ticks.tick(3, 0)
        scatter_two.arrived()
        scatter_two.done()

    pl.run_scoped(
        normed_grads, V((d, 3 * cols), BF16), V((3, local, d), BF16), V((local, d), BF16)
    )

    def first_norm_back(at, back):
        gm[at, :] += back

    norm_back_rows(
        local, gain_one, lambda at: x_ref[at, :].astype(F32), summed, gp, 0, first_norm_back
    )
    results = [
        pltpu.make_async_copy(
            gm.at[:, own_columns(*p)], input_grad_out.at[:, true_columns(*p)], sem_in.at[n]
        )
        for n, p in enumerate(sides)
    ]
    for copy in results:
        copy.start()
    peers = [me.x, me.y] + [{"dp": (me.index + k) % dp} for k in range(1, dp)]
    exchange = [
        remote(gp, gp_landed.at[n], sem_gain.at[n, 0], sem_gain.at[n, 1], device)
        for n, device in enumerate(peers)
    ]
    for n in range(2):
        exchange[n].start()
        exchange[n].wait()
        gp[...] += gp_landed[n]
    for copy in exchange[2:]:
        copy.start()
    ticks.rest()
    for copy in exchange[2:]:
        copy.wait()
    for k in range(1, dp):
        if k % 2 == 1:
            gp[:, :half] += gp_landed[1 + k, :, half:]
            gp[:, half:] += gp_landed[1 + k, :, :half]
        else:
            gp[...] += gp_landed[1 + k]
    gain_out[...] = gp[...]
    ticks.done()
    pl.semaphore_wait(free_core, 1)
    for k in range(1, dp):
        gain_copy(k, me.index).wait_send()
    for copy in results:
        copy.wait()
    for one in [wa, wo, square] + gathers:
        one.done()


def layer(dp, x, g, gains, wq, wk, wv, wo, gate, up, down, docs):
    line = dp // 2
    local, d = x.shape
    cols, ff = wq.shape[1], gate.shape[1]
    blocks, shard = FF_BLOCKS, d // dp
    fw = ff // blocks
    groups = cols // GROUP
    count = blocks + 1 + groups
    most = max(3 * fw, cols, 3 * GROUP)
    vm, hbm = pl.BlockSpec(memory_space=pltpu.VMEM), pl.BlockSpec(memory_space=pl.ANY)
    S, V, dma = jax.ShapeDtypeStruct, pltpu.VMEM, pltpu.SemaphoreType.DMA
    regular = pltpu.SemaphoreType.REGULAR
    slab = S((LEN, cols), BF16)
    piece = V((line, most, shard), BF16)
    return pl.pallas_call(
        functools.partial(layer_kernel, dp),
        in_specs=[hbm, hbm, vm, hbm, hbm, hbm, vm, hbm, hbm, vm, vm],
        out_specs=[hbm, hbm, vm] + [hbm] * 24,
        out_shape=[
            S((local, d), BF16), S((local, d), F32), S((8, d), F32),
            S((shard, ff), BF16), S((shard, ff), BF16), S((ff, shard), BF16),
            S((shard, cols), BF16), S((shard, cols), BF16), S((shard, cols), BF16), S((cols, shard), BF16),
            S((2, d // 2, 3 * cols), BF16), S((2, d // 2, cols), BF16),
            S((blocks, 2, d // 2, 3 * fw), BF16), S((blocks, LEN, fw), BF16),
            S((count, line, most, shard), BF16), S((count, line + 1, most, shard), BF16),
            S((LEN, d), BF16), S((LEN, d), BF16), slab, slab, slab, S((cols, LEN), BF16), S((LEN, 128), F32),
            S((LEN, 128), F32), S((LEN, 128), F32), S((LEN, 128), jnp.int32), S((4, 8, LEN // 4), jnp.int32),
        ],
        scratch_shapes=[
            V((local, d), BF16), V((shard, 3 * cols), BF16), V((shard, cols), BF16),
            V((blocks, shard, 3 * fw), BF16), V((2, line * 16, shard), BF16),
            V((LEN, d), BF16), V((LEN, d), BF16), V((LEN, d), BF16),
            piece, piece, piece, V((9, most, shard), BF16), V((most, shard), F32), V((3, shard, 256), BF16),
            V((3, local, d), BF16), V((3, local, d), BF16), V((local, d), F32), V((local, d), F32),
            V((local, d), F32), V((8, d), F32), V((dp + 1, 8, d), F32),
            dma((4 * line + 3 + 2 * blocks,)), dma((2, dp)), dma((6, line)), dma((6, line)),
            dma((blocks, 6, line)), dma((8,)), dma((8,)), dma((8,)), dma((8,)), dma((12,)),
            dma((count, 2 * line + 1)), dma((12,)), dma((3,)), dma((dp + 1, 2)), dma((3 * blocks,)), dma((2, 2)),
            regular, regular, regular,
        ],
        compiler_params=pltpu.CompilerParams(
            vmem_limit_bytes=VMEM_BYTES, collective_id=0, has_side_effects=True
        ),
        name="layer",
    )(x, g, gains, wq, wk, wv, wo, gate, up, down, docs)


def widen_kernel(*refs):
    count = (len(refs) - 2) // 4
    ins, outs = refs[:count], refs[count : 2 * count]
    here, wide = refs[2 * count : 3 * count], refs[3 * count : 4 * count]
    sem_in, sem_out = refs[-2:]
    loads = [pltpu.make_async_copy(a, b, sem_in.at[n]) for n, (a, b) in enumerate(zip(ins, here))]
    stores = [pltpu.make_async_copy(a, b, sem_out.at[n]) for n, (a, b) in enumerate(zip(wide, outs))]
    for copy in loads:
        copy.start()
    for n, (load, store) in enumerate(zip(loads, stores)):
        load.wait()
        rows = here[n].shape[0]
        step = min(rows, 64)

        @pl.loop(0, rows // step)
        def _(i, n=n, step=step):
            at = pl.ds(pl.multiple_of(i * step, step), step)
            wide[n][at, :] = here[n][at, :].astype(wide[n].dtype)

        store.start()
    for store in stores:
        store.wait()


def widen(arrays, dtypes):
    hbm = pl.BlockSpec(memory_space=pl.ANY)
    return pl.pallas_call(
        widen_kernel,
        in_specs=[hbm] * len(arrays),
        out_specs=[hbm] * len(arrays),
        out_shape=[jax.ShapeDtypeStruct(a.shape, t) for a, t in zip(arrays, dtypes)],
        scratch_shapes=[pltpu.VMEM(a.shape, a.dtype) for a in arrays]
        + [pltpu.VMEM(a.shape, t) for a, t in zip(arrays, dtypes)]
        + [pltpu.SemaphoreType.DMA((len(arrays),))] * 2,
        compiler_params=pltpu.CompilerParams(vmem_limit_bytes=VMEM_BYTES),
        name="widen",
    )(*arrays)


def on_device(
    dp, tensor, hidden_in, doc_lengths, gain_attn, w_query, w_key, w_value, w_out, gain_mlp,
    w_gate, w_up, w_down, cotangent,
):
    line = dp // 2
    core = lax.axis_index("dp") % 2
    place = lax.axis_index("tensor")
    square = tensor == 4 and dp == 8
    same_core = [[c + 2 * z for z in range(line)] for c in range(2)]
    sibling = [(i, i ^ 1) for i in range(dp)]
    d = hidden_in.shape[1]
    local = hidden_in.shape[0]

    def own_first(a):
        s = a.reshape(a.shape[:-1] + (line, 2, d // dp))
        even, odd = s[..., 0, :], s[..., 1, :]
        out = jnp.concatenate(
            [jnp.where(core == 0, even, odd), jnp.where(core == 0, odd, even)], axis=-2
        )
        return out.reshape(a.shape)

    def true_order(a):
        s = a.reshape(a.shape[:-1] + (2, line, d // dp))
        first, second = s[..., 0, :, :], s[..., 1, :, :]
        out = jnp.stack(
            [jnp.where(core == 0, first, second), jnp.where(core == 0, second, first)], axis=-2
        )
        return out.reshape(a.shape)

    def hop(a, step):
        return lax.ppermute(a, "tensor", [(i, i ^ step) for i in range(tensor)])

    def gather_rows(a):
        if not square:
            return lax.all_gather(a, "tensor", axis=0, tiled=True)
        half = a.shape[0] // 2
        from_x, from_y = hop(a, 1), hop(a, 2)
        top, bottom = hop(from_x[:half], 2), hop(from_y[half:], 1)
        return jnp.concatenate([a, from_x, from_y, top, bottom], axis=0)

    def scatter_rows(a):
        if not square:
            return lax.psum_scatter(a, "tensor", scatter_dimension=0, tiled=True).astype(F32)
        n = a.shape[0] // 4
        half = n // 2
        top = hop(a[3 * n : 3 * n + half], 2)
        bottom = hop(a[3 * n + half :], 1)
        for_x = jnp.concatenate([a[n : n + half] + top, a[n + half : 2 * n]], axis=0)
        for_y = jnp.concatenate([a[2 * n : 2 * n + half], a[2 * n + half : 3 * n] + bottom], axis=0)
        return (a[:n].astype(F32) + hop(for_x, 1).astype(F32)) + hop(for_y, 2).astype(F32)

    def line_gather(a):
        own = lax.all_gather(a, "dp", axis=0, axis_index_groups=same_core, tiled=True)
        return own, lax.ppermute(own, "dp", sibling)

    def line_scatter(own, sib):
        mine = own + lax.ppermute(sib, "dp", sibling)
        return lax.psum_scatter(
            mine, "dp", scatter_dimension=0, axis_index_groups=same_core, tiled=True
        ).astype(F32)

    blocks = 4
    rows = LEN // blocks
    key = place if square else jnp.zeros((), jnp.int32)
    tokens = (
        (jnp.arange(blocks, dtype=jnp.int32) ^ key)[:, None] * rows
        + jnp.arange(rows, dtype=jnp.int32)[None, :]
    ).reshape(LEN)
    segment, position = doc_tables(doc_lengths, tokens)
    cosine, sine = rotary_tables(position)
    segc = jnp.broadcast_to(segment[:, None], (LEN, 128))
    segr = jnp.broadcast_to(segment.reshape(blocks, 1, rows), (blocks, 8, rows))
    key = key.reshape(1)
    cols = w_query.shape[1]
    if square:
        gain_rows = jnp.pad(
            jnp.concatenate([gain_attn, gain_mlp]), (0, 14 * gain_attn.shape[0])
        ).reshape(16, -1)
        (
            output, input_grad, gain_sum, grad_gate, grad_up, grad_down, grad_query, grad_key,
            grad_value, grad_out, *_,
        ) = layer(
            dp, hidden_in, cotangent, gain_rows, w_query, w_key, w_value, w_out, w_gate, w_up,
            w_down, doc_lengths,
        )
        share = d // (dp * tensor)
        first = (lax.axis_index("dp") // 2) * (d // dp) + place * share
        gain_sum = lax.dynamic_slice_in_dim(gain_sum, first, share, 1)
        grads = (grad_gate, grad_up, grad_down, grad_query, grad_key, grad_value, grad_out)
        (
            output, input_grad, grad_gate, grad_up, grad_down, grad_query, grad_key, grad_value, grad_out
        ) = widen((output, input_grad) + grads, (BF16,) + (F32,) * 8)
        return (
            output, input_grad, gain_sum[0], grad_query, grad_key, grad_value, grad_out, gain_sum[1],
            grad_gate, grad_up, grad_down,
        )

    cosine, sine = (jnp.tile(a, (1, GROUP // 128)) for a in (cosine, sine))
    ff = w_gate.shape[1]
    fb = ff // FF_BLOCKS
    down_t = w_down.T
    shards = [
        jnp.concatenate([w[:, b * fb : (b + 1) * fb] for w in (w_gate, w_up, down_t)], axis=1)
        for b in range(FF_BLOCKS)
    ]
    qkv_shard = jnp.concatenate([w_query, w_key, w_value], axis=1)
    g_local = own_first(cotangent)
    inputs = own_first(hidden_in).astype(F32)
    factor_one = norm_factor(inputs)
    gains = lax.all_gather(jnp.stack([gain_attn, gain_mlp]), "dp", axis=0)
    gains = own_first(jnp.moveaxis(gains, 0, 1).reshape(2, d)).astype(F32)
    gain_one, gain_two = gains[0], gains[1]
    qkv_own, qkv_sib = line_gather(qkv_shard)
    out_own, out_sib = line_gather(w_out.T)
    normed = gather_rows((inputs * factor_one * gain_one).astype(BF16))
    g_all = gather_rows(g_local)
    query, keys, values, mixed, lse = attn_forward(
        blocks, key, normed, qkv_own, qkv_sib, cosine, sine, segc, segr
    )
    attended = jnp.concatenate(
        [dot_nt(mixed, out_own).astype(BF16), dot_nt(mixed, out_sib).astype(BF16)], axis=1
    )
    middle = inputs + scatter_rows(attended)
    factor_two = norm_factor(middle)
    normed_mlp = gather_rows((middle * factor_two * gain_two).astype(BF16))
    ff_sets = [jnp.concatenate(line_gather(shard), axis=0) for shard in shards]

    down_sum = jnp.zeros((LEN, d), F32)
    back_sum = jnp.zeros((LEN, d), F32)
    ff_grads = []
    for b in range(FF_BLOCKS):
        gate_w, up_w, down_w = jnp.split(ff_sets[b], 3, axis=1)
        gate_pre = dot_nn(normed_mlp, gate_w)
        upward = dot_nn(normed_mlp, up_w)
        grad_hidden = dot_nn(g_all, down_w)
        sig = jax.nn.sigmoid(gate_pre)
        activated = gate_pre * sig
        hidden = (activated * upward).astype(BF16)
        grad_gate_pre = (grad_hidden * upward * sig * (1.0 + gate_pre * (1.0 - sig))).astype(BF16)
        grad_upward = (grad_hidden * activated).astype(BF16)
        down_sum = down_sum + dot_nt(hidden, down_w)
        back_sum = back_sum + dot_nt(grad_gate_pre, gate_w) + dot_nt(grad_upward, up_w)
        grad = jnp.concatenate(
            [
                dot_tn(normed_mlp, grad_gate_pre).astype(BF16),
                dot_tn(normed_mlp, grad_upward).astype(BF16),
                dot_tn(g_all, hidden).astype(BF16),
            ],
            axis=1,
        )
        ff_grads.append(line_scatter(grad[: d // 2], grad[d // 2 :]))
    grad_norm_two = scatter_rows(back_sum.astype(BF16))
    output = true_order((middle + scatter_rows(down_sum.astype(BF16))).astype(BF16))
    grad_mid_norm, gain_two_part = norm_back(middle, factor_two, gain_two, grad_norm_two)
    grad_middle = g_local.astype(F32) + grad_mid_norm
    grad_mid_all = gather_rows(grad_middle.astype(BF16))

    dq, dk, dv = attn_backward(
        blocks, key, grad_mid_all, out_own, out_sib, query, keys, values, lse, cosine, sine,
        segc, segr,
    )
    grad = jnp.concatenate(
        [dot_tn(normed, dq), dot_tn(normed, dk), dot_tn(normed, dv), dot_tn(grad_mid_all, mixed)],
        axis=1,
    ).astype(BF16)
    attn_grads = line_scatter(grad[: d // 2], grad[d // 2 :])
    rows_grad = jnp.concatenate([dq, dk, dv], axis=1)
    back = jnp.concatenate(
        [
            dot_nt(rows_grad, qkv_own).astype(BF16),
            dot_nt(rows_grad, qkv_sib).astype(BF16),
        ],
        axis=1,
    )
    grad_in_norm, gain_one_part = norm_back(inputs, factor_one, gain_one, scatter_rows(back))
    input_grad = true_order(grad_middle + grad_in_norm)

    parts = true_order(jnp.stack([gain_one_part, gain_two_part])).reshape(2 * d)
    shares = lax.all_gather(parts, ("dp", "tensor"), axis=0)
    gain_sum = jnp.sum(shares, axis=0).reshape(2, d)
    share = d // (dp * tensor)
    first = (lax.axis_index("dp") * tensor + place) * share
    gain_sum = lax.dynamic_slice_in_dim(gain_sum, first, share, 1)

    return (
        output,
        input_grad,
        gain_sum[0],
        attn_grads[:, :cols],
        attn_grads[:, cols : 2 * cols],
        attn_grads[:, 2 * cols : 3 * cols],
        attn_grads[:, 3 * cols :].T,
        gain_sum[1],
        jnp.concatenate([g[:, :fb] for g in ff_grads], axis=1),
        jnp.concatenate([g[:, fb : 2 * fb] for g in ff_grads], axis=1),
        jnp.concatenate([g[:, 2 * fb :] for g in ff_grads], axis=1).T,
    )


def solution(mesh):
    shape = dict(mesh.shape)
    return jax.shard_map(
        functools.partial(on_device, shape["dp"], shape["tensor"]),
        mesh=mesh,
        in_specs=(
            P(("dp", "tensor"), None),
            P("dp", None),
            P("dp"),
            P("dp", "tensor"),
            P("dp", "tensor"),
            P("dp", "tensor"),
            P("tensor", "dp"),
            P("dp"),
            P("dp", "tensor"),
            P("dp", "tensor"),
            P("tensor", "dp"),
            P(("dp", "tensor"), None),
        ),
        out_specs=(
            P(("dp", "tensor"), None),
            P(("dp", "tensor"), None),
            P(("dp", "tensor")),
            P("dp", "tensor"),
            P("dp", "tensor"),
            P("dp", "tensor"),
            P("tensor", "dp"),
            P(("dp", "tensor")),
            P("dp", "tensor"),
            P("dp", "tensor"),
            P("tensor", "dp"),
        ),
        check_vma=False,
    )
```

profile of v0, /device:TPU:0, one launch (start us, length us, event | category | flops | bytes accessed | tf_op | source)
XLA Modules:
  0.0 490.4 jit_solution(6149570995408596410)
XLA Ops:
  0.6 0.7 fusion.2
  1.3 0.6 reshape.25.gain_ref
  1.9 480.9 %layer.1 = (bf16[256,2048]{1,0:T(8,128)(2,1)}, f32[256,2048]{1,0:T(8,128)}, f32[8,2048]{1,0:T(8,128)}, bf16[256,2048]{1,0:T(8,128)(2,1)}, bf16[256,2048]{1,0:T(8...) custom-call(bf16[256,2048]{1,0:T(8,128)(2,1)} %x_in.1, ...), custom_call_target="tpu_custom_call" | custom-call | tf_op jit(solution)/shard_map/layer/pallas_call | solution.py:1493
  482.8 6.1 %widen.1 = (bf16[256,2048]{1,0:T(8,128)(2,1)}, f32[256,2048]{1,0:T(8,128)}, f32[256,2048]{1,0:T(8,128)}, f32[256,2048]{1,0:T(8,128)}, f32[2048,256]{1,0:T(8,128)...) custom-call(bf16[256,2048]{1,0:T(8,128)(2,1)} %get-tuple-element.30.refs_0_, ...), custom_call_target="tpu_custom_call" | custom-call | tf_op jit(solution)/shard_map/widen/pallas_call | solution.py:1552
  489.0 0.8 constant_dynamic-slice_fusion
  489.7 0.5 slice_bitcast_fusion
where the time goes:
time: 497 us; the launch traced here: 490 us
  Pallas kernels  487 us (98%)
    pallas_call x1, Pallas kernels, layer(): pl.pallas_call(functools.partial(layer_kernel, dp), in_specs=[hbm, hbm, v...  481 us

commit v1 on v0

--- a/solution.py
+++ b/solution.py
@@ -385,10 +385,12 @@
         copies[0].start()
         copies[1].start()
 
+    def side_ready(self, slot):
+        self.copies()[2 + slot].start()
+
     def sides_ready(self):
-        copies = self.copies()
-        copies[2].start()
-        copies[3].start()
+        self.side_ready(0)
+        self.side_ready(1)
 
     def combine(self):
         copies = self.copies()
@@ -948,8 +950,10 @@
         copy.wait()
     normed.forward()
     grads.start()
-    poll(line - 2)
+    poll(line - 3)
     normed.arrived()
+    pl.when(me.at_end)(grads.forward)
+    poll()
     wa.arrived()
 
     def free_landed():
@@ -1003,55 +1007,53 @@
         for copy in stores:
             copy.start()
         poll(2)
-        for i in range(4):
-            places = [(j, me.spots[j]) for j in key_blocks(i, rows)]
-            at = at_block(me.spots[i])
-            fill_bias(bias_ref, segc_ref[at, 0:1], segr_ref, i, places)
-            spots = [at_block(p) for _, p in places]
+        def queries(p):
+            at = pl.ds(p * rows, rows)
+            spots = me.window(me.spots[p], rows, segc_ref[at, 0:1], segr_ref, bias_ref)
 
             @pl.loop(0, cols // 128)
-            def _(pair, at=at, spots=spots):
+            def _(pair):
                 attend(pair, 0, at, spots, head_lane, q_ref, k_ref, v_ref, mixed_ref, lse_ref, bias_ref)
 
-            if i == 0:
-                poll(line - 3)
-            if i == 1:
-                grads.forward()
-            if i == 2:
-                wo.arrived()
-                wo_load = [
-                    pltpu.make_async_copy(wo_full.at[side], wo_v.at[pl.ds(side * half, half)], sem_w.at[0, side])
-                    for side in range(2)
-                ]
-                for copy in wo_load:
-                    copy.start()
-                poll()
-        mixed_t[...] = mixed_ref[...].T
-        for n, (a, b) in enumerate(((mixed_t, mixed_all), (lse_ref, lse_all))):
-            stores.append(pltpu.make_async_copy(a, b, sem_c.at[len(outs) + n]))
-            stores[-1].start()
-        for copy in wo_load:
-            copy.wait()
-
-        def out_rows(b, slot, count=1):
-            at = pl.ds(b * rows, count * rows)
+        def out_rows(b, slot):
+            at = pl.ds(b * rows, rows)
             for side in range(2):
                 here = pl.ds(side * half, half)
                 value = dot_nt(mixed_ref[at, :], wo_v[here, :])
                 if slot is None:
                     own[:, here] = value
                 else:
-                    for k in range(count):
-                        stage[slot + k, :, here] = value[k * rows : (k + 1) * rows].astype(BF16)
-
+                    stage[slot, :, here] = value.astype(BF16)
+
+        queries(3)
+        poll(line - 3)
+        queries(1)
+        wo.arrived()
+        wo_load = [
+            pltpu.make_async_copy(wo_full.at[side], wo_v.at[pl.ds(side * half, half)], sem_w.at[0, side])
+            for side in range(2)
+        ]
+        for copy in wo_load:
+            copy.start()
+        pl.when(jnp.logical_not(me.at_end))(grads.forward)
+        for copy in wo_load:
+            copy.wait()
         out_rows(3, 2)
         scatter.diagonal_ready()
-        out_rows(1, 0, 2)
-        scatter.sides_ready()
+        out_rows(1, 0)
+        scatter.side_ready(0)
+        queries(2)
+        out_rows(2, 1)
+        scatter.side_ready(1)
+        poll()
+        queries(0)
+        mixed_t[...] = mixed_ref[...].T
+        for n, (a, b) in enumerate(((mixed_t, mixed_all), (lse_ref, lse_all))):
+            stores.append(pltpu.make_async_copy(a, b, sem_c.at[len(outs) + n]))
+            stores[-1].start()
         out_rows(0, None)
-        poll()
         scatter.combine()
-        poll(3)
+        poll(4)
         for copy in stores:
             copy.wait()
         normed.done()

time: 497 us -> 498 us (level)
  no operation moved by 1% of the time
where the time goes in v1:
time: 498 us; the launch traced here: 490 us
  Pallas kernels  487 us (98%)
    pallas_call x1, Pallas kernels, layer(): pl.pallas_call(functools.partial(layer_kernel, dp), in_specs=[hbm, hbm, v...  481 us

profile of v1, /device:TPU:0, one launch (start us, length us, event | category | flops | bytes accessed | tf_op | source)
XLA Modules:
  0.0 490.2 jit_solution(442586731837014768)
XLA Ops:
  0.6 0.7 fusion.2
  1.3 0.6 reshape.25.gain_ref
  1.9 480.6 %layer.1 = (bf16[256,2048]{1,0:T(8,128)(2,1)}, f32[256,2048]{1,0:T(8,128)}, f32[8,2048]{1,0:T(8,128)}, bf16[256,2048]{1,0:T(8,128)(2,1)}, bf16[256,2048]{1,0:T(8...) custom-call(bf16[256,2048]{1,0:T(8,128)(2,1)} %x_in.1, ...), custom_call_target="tpu_custom_call" | custom-call | tf_op jit(solution)/shard_map/layer/pallas_call | solution.py:1495
  482.5 6.1 %widen.1 = (bf16[256,2048]{1,0:T(8,128)(2,1)}, f32[256,2048]{1,0:T(8,128)}, f32[256,2048]{1,0:T(8,128)}, f32[256,2048]{1,0:T(8,128)}, f32[2048,256]{1,0:T(8,128)...) custom-call(bf16[256,2048]{1,0:T(8,128)(2,1)} %get-tuple-element.30.refs_0_, ...), custom_call_target="tpu_custom_call" | custom-call | tf_op jit(solution)/shard_map/widen/pallas_call | solution.py:1554
  488.7 0.8 constant_dynamic-slice_fusion
  489.4 0.5 slice_bitcast_fusion
